TPU v7x, 128 devices: a whole 4x4x4 slice. The times are simulated.
128 devices in a mesh: orbit: 2 (over core), scene: 16 (over y, x), shard: 4 (over z).
Axes of the slice: x: 4, y: 4, z: 4, core: 2. Of those that a mesh axis runs over, the one named last changes fastest.
Arguments:
- sigma0: bfloat16 [2, 131072, 256], P('orbit', ('scene', 'shard')), may hold values from 0.0001 to 32
- area_tiles: bfloat16 [65536, 256], P(('orbit', 'scene')), may hold values from 0.3984375 to 2.5
- tile_owner: int32 [2, 131072, 1], P('orbit', ('scene', 'shard')), may hold values from 0 to 31; in each aligned block of 2048 rows (0 to 2047, 2048 to 4095, ..., all dimensions but the last counted through in order) at most 128 rows name the same one
- tile_slot: int32 [2, 131072], P('orbit', ('scene', 'shard')), may hold values from 0 to 2047
- trainer_band: int32 [2, 131072, 1], P('orbit', ('scene', 'shard')), may hold values from 0 to 63; in each aligned block of 2048 rows (0 to 2047, 2048 to 4095, ..., all dimensions but the last counted through in order) at most 64 rows name the same one
- seam_offset: int32 [2, 64], P('orbit', ('scene', 'shard')), may hold values from 0 to 63
Outputs:
- patches: float32 [2, 262144, 256], P('orbit', ('scene', 'shard'))
Inputs may be any that keep to these rules, and one draw needn't show every extreme that they name: `tile_owner`: within the 2048 rows of one block of one orbit group no owner is named by more than 128 rows, a bound that some block reaches. `trainer_band`: within the 2048 rows of one block of one orbit group no band is named by more than 64 rows, a bound that some block reaches.
All inputs are finite; a program needn't handle non-finite values.
Results may differ from a plain program's by a relative error of at most 0.0025.
Values may be sent and summed in bfloat16 or wider, within the bound.
A program may use at most 64 MiB of HBM per device.

v0:
```python
import math

import jax
import jax.numpy as jnp
from jax import lax
from jax.sharding import PartitionSpec as P

NOISE = 0.25


def with_halo(cells, sides, width):
    for axis, dim in sides:
        count = lax.axis_size(axis)
        ends = count - 1
        head = lax.slice_in_dim(cells, 0, width, axis=dim)
        tail = lax.slice_in_dim(cells, cells.shape[dim] - width, cells.shape[dim], axis=dim)
        cells = jnp.concatenate(
            [
                lax.ppermute(tail, axis, [(i, (i + 1) % count) for i in range(ends)]),
                cells,
                lax.ppermute(head, axis, [((i + 1) % count, i) for i in range(ends)]),
            ],
            axis=dim,
        )
    return cells


def window_sum(padded, count_rows, pixels):
    vertical = padded[0:count_rows]
    for offset in range(1, 7):
        vertical = vertical + padded[offset : offset + count_rows]
    widened = jnp.pad(vertical, ((0, 0), (3, 3)))
    window = widened[:, 0:pixels]
    for offset in range(1, 7):
        window = window + widened[:, offset : offset + pixels]
    return window


def lee_filter(intensity, first_row, all_rows):
    count_rows = intensity.shape[0] - 6
    pixels = intensity.shape[1]
    center = intensity[3 : 3 + count_rows]
    first_sum = window_sum(intensity, count_rows, pixels)
    second = window_sum(intensity * intensity, count_rows, pixels)
    line_idx = first_row + jnp.arange(count_rows, dtype=jnp.int32)
    row_span = jnp.minimum(line_idx + 3, all_rows - 1) - jnp.maximum(line_idx - 3, 0) + 1
    column = jnp.arange(pixels, dtype=jnp.int32)
    col_span = jnp.minimum(column + 3, pixels - 1) - jnp.maximum(column - 3, 0) + 1
    counts = (row_span[:, None] * col_span[None, :]).astype(jnp.float32)
    local_mean = first_sum / counts
    variance = second / counts - local_mean * local_mean
    speckle = NOISE * local_mean * local_mean
    mixing = jnp.maximum(variance - speckle, 0.0) / (variance + speckle)
    return local_mean + mixing * (center - local_mean)


def rank_within(labels, number):
    rows = labels.shape[0]
    block = math.gcd(rows, 128)
    onehot = (labels[:, None] == jnp.arange(number, dtype=jnp.int32)[None, :]).astype(jnp.bfloat16)
    blocks = onehot.reshape(rows // block, block, number)
    lower = (
        jnp.arange(block, dtype=jnp.int32)[:, None] > jnp.arange(block, dtype=jnp.int32)[None, :]
    ).astype(jnp.bfloat16)
    within = jnp.einsum("ij,bjn->bin", lower, blocks, preferred_element_type=jnp.float32)
    totals = jnp.sum(blocks.astype(jnp.float32), axis=1)
    offsets = jnp.cumsum(totals, axis=0) - totals
    before = (within + offsets[:, None, :]).reshape(rows, number)
    order = jnp.sum(before * onehot.astype(jnp.float32), axis=1).astype(jnp.int32)
    return (order, jnp.sum(totals, axis=0).astype(jnp.int32))


def place_rows(target, values, total):
    block = math.gcd(total, 1024)

    def place_one_block(start):
        slots = start + jnp.arange(block, dtype=jnp.int32)
        picker = (slots[:, None] == target[None, :]).astype(jnp.bfloat16)
        return jnp.dot(picker, values, preferred_element_type=jnp.float32).astype(jnp.bfloat16)

    starts = jnp.arange(total // block, dtype=jnp.int32) * block
    placed = lax.map(place_one_block, starts)
    return placed.reshape(total, values.shape[1])


def pick_rows(source, table):
    rows = source.shape[0]
    block = math.gcd(rows, 1024)
    entries = jnp.arange(table.shape[0], dtype=jnp.int32)

    def pick_one_block(wanted):
        picker = (wanted[:, None] == entries[None, :]).astype(jnp.bfloat16)
        return jnp.dot(picker, table, preferred_element_type=jnp.float32).astype(jnp.bfloat16)

    picked = lax.map(pick_one_block, source.reshape(rows // block, block))
    return picked.reshape(rows, table.shape[1])


def per_device(sigma0, area_tiles, tile_owner, tile_slot, trainer_band, seam_offset):
    local_rows = sigma0.shape[1]
    pixels = sigma0.shape[2]
    trainers = lax.axis_size(("scene", "shard"))
    padded = with_halo(sigma0, ((("scene", "shard"), 1),), 3)
    first_row = lax.axis_index(("scene", "shard")) * local_rows
    filtered = lee_filter(padded[0].astype(jnp.float32), first_row, local_rows * trainers)
    owner_id = tile_owner[0, :, 0]
    tile_pos = tile_slot[0]
    owners = lax.axis_size(("orbit", "scene"))
    capacity = 2 * local_rows // owners
    order_in = rank_within(owner_id, owners)[0]
    request = jnp.zeros((owners, capacity), jnp.int32).at[owner_id, order_in].set(tile_pos)
    looked_up = jnp.take(
        area_tiles,
        lax.all_to_all(request, ("orbit", "scene"), split_axis=0, concat_axis=0, tiled=True),
        axis=0,
    )
    replies = lax.all_to_all(looked_up, ("orbit", "scene"), split_axis=0, concat_axis=0, tiled=True)
    weight = pick_rows(owner_id * capacity + order_in, replies.reshape(owners * capacity, pixels))
    flat = (filtered * weight.astype(jnp.float32)).astype(jnp.bfloat16)
    trainer = (trainer_band[0, :, 0] + seam_offset[0, 0]) % trainers
    slot_cap = 2 * local_rows // trainers
    order_out, per_trainer = rank_within(trainer, trainers)
    outgoing = place_rows(trainer * slot_cap + order_out, flat, trainers * slot_cap).reshape(
        trainers, slot_cap, pixels
    )
    incoming, arrived = (
        lax.all_to_all(outgoing, ("scene", "shard"), split_axis=0, concat_axis=0, tiled=True),
        lax.all_to_all(per_trainer, ("scene", "shard"), split_axis=0, concat_axis=0, tiled=True),
    )
    filled = jnp.arange(slot_cap, dtype=jnp.int32)[None, :] < arrived[:, None]
    safe_vals = jnp.where(filled[:, :, None], incoming.astype(jnp.float32), 1.0)
    patches = jnp.where(filled[:, :, None], jnp.log(safe_vals), 0.0)
    return patches.reshape(1, trainers * slot_cap, pixels)


def solution(mesh):
    return jax.shard_map(
        per_device,
        mesh=mesh,
        in_specs=(
            P("orbit", ("scene", "shard"), None),
            P(("orbit", "scene"), None),
            P("orbit", ("scene", "shard"), None),
            P("orbit", ("scene", "shard")),
            P("orbit", ("scene", "shard"), None),
            P("orbit", ("scene", "shard")),
        ),
        out_specs=P("orbit", ("scene", "shard"), None),
        check_vma=False,
    )
```

profile of v0, /device:TPU:1, one launch (start us, length us, event | category | flops | bytes accessed | tf_op | source)
XLA Modules:
  0.0 193.3 jit_solution(10936607042314446173)
XLA Ops:
  4.3 8.8 %scatter_custom_fusion = s32[4096]{0:T(1024)} fusion(s32[2048]{0:T(1024)S(1)} %broadcast_select_fusion.1, s32[2048]{0:T(1024)} %bitcast.107, s32[]{:T(128)} %constant.43.clone.1), kind=kCustom, calls=%fused_computation.109 | custom fusion | bytes 16896
  13.1 8.6 %all-to-all-start.1 = ((s32[32,1,128]{2,1,0:T(1,128)}), s32[32,1,128]{2,1,0:T(1,128)S(1)}, u32[]{:S(2)}, u32[]{:S(2)}) async-start(s32[32,1,128]{2,1,0:T(1,128)} %bitcast.20), calls=%async_computation.1 | async-start | bytes 32768 | tf_op jit(solution)/shard_map/all_to_all | solution.py:114
  22.4 3.5 %collective-permute-start = (bf16[1,3,256]{2,1,0:T(4,128)(2,1)S(1)}, bf16[1,3,256]{2,1,0:T(4,128)(2,1)S(1)}, u32[]{:S(2)}, u32[]{:S(2)}) collective-permute-start(bf16[1,3,256]{2,1,0:T(4,128)(2,1)S(1)} %get-tuple-element.92), channel_id=1, source_target_pairs={{0,1},{1,2},{2,3},{3,4},{4,5},{5,6},{6,7},{7,8},{8,9},{9,10},{10,1... | collective-permute-start | bytes 4616 | tf_op jit(solution)/shard_map/ppermute | solution.py:19
  30.8 7.0 %concatenate.6 = bf16[1,2054,256]{2,1,0:T(8,128)(2,1)} concatenate(bf16[1,3,256]{2,1,0:T(4,128)(2,1)S(1)} %collective-permute-done, bf16[1,2048,256]{2,1,0:T(8,128)(2,1)S(1)} %copy-done.2, bf16[1,3,256]{2,1,0:T(4,128)(2,1)S(1)} %collective-permute-done.1), dimensions={1} | concatenate | bytes 2103296 | tf_op jit(solution)/shard_map/concatenate | solution.py:17
  37.7 1.4 convert_element_type.94
  39.2 16.9 %gather_fusion = bf16[4096,256]{1,0:T(8,128)(2,1)} fusion(bf16[2048,256]{1,0:T(8,128)(2,1)S(1)} %copy-done, s32[4096]{0:T(1024)S(1)} %fusion.56), kind=kCustom, calls=%fused_computation | custom fusion | bytes 4210688 | tf_op jit(solution)/shard_map/jit(_take)/gather | solution.py:112
  56.1 2.9 %broadcast_select_fusion = bf16[32,128,256]{2,1,0:T(8,128)(2,1)} fusion(bf16[32,128,256]{2,1,0:T(8,128)(2,1)} %bitcast.97, pred[32,128]{1,0:T(8,128)(4,1)S(1)} %compare_and_fusion), kind=kLoop, calls=%fused_computation.67 | loop fusion | flops 1048576 | bytes 4198400 | tf_op jit(solution)/shard_map/jit(_take)/select_n | solution.py:112
  59.0 10.5 %all-to-all-start.2 = ((bf16[32,128,256]{2,1,0:T(8,128)(2,1)}), bf16[32,128,256]{2,1,0:T(8,128)(2,1)}, u32[]{:S(2)}, u32[]{:S(2)}) async-start(bf16[32,128,256]{2,1,0:T(8,128)(2,1)} %broadcast_select_fusion), calls=%async_computation.2 | async-start | bytes 4194304 | tf_op jit(solution)/shard_map/all_to_all | solution.py:117
  69.6 2.6 %fusion.36 = f32[2048,256]{1,0:T(8,128)} fusion(f32[1,2054,256]{2,1,0:T(8,128)S(1)} %convert_element_type.94), kind=kLoop, calls=%fused_computation.55 | loop fusion | flops 3145728 | bytes 16777216 | tf_op jit(solution)/shard_map/add | solution.py:31
  72.3 2.5 %fusion.35 = f32[2048,256]{1,0:T(8,128)} fusion(f32[1,2054,256]{2,1,0:T(8,128)S(1)} %convert_multiply_fusion.1), kind=kLoop, calls=%fused_computation.48 | loop fusion | flops 3145728 | bytes 16777216 | tf_op jit(solution)/shard_map/add | solution.py:31
  74.8 23.2 %all-to-all-done.2 = bf16[32,128,256]{2,1,0:T(8,128)(2,1)} async-done(((bf16[32,128,256]{2,1,0:T(8,128)(2,1)}), bf16[32,128,256]{2,1,0:T(8,128)(2,1)}, u32[]{:S(2)}, u32[]{:S(2)}) %all-to-all-start.2) | async-done | bytes 2097184 | tf_op jit(solution)/shard_map/all_to_all | solution.py:117
  98.0 7.7 %all-to-all-start = ((s32[64,1,1]{2,1,0:T(1,128)}), s32[64,1,1]{2,1,0:T(1,128)S(1)}, u32[]{:S(2)}, u32[]{:S(2)}) async-start(s32[64,1,1]{2,1,0:T(1,128)} %copy.8), calls=%async_computation | async-start | bytes 65536 | tf_op jit(solution)/shard_map/all_to_all | solution.py:128
  105.8 10.6 %while.22 = (s32[]{:T(128)}, bf16[2,1024,256]{2,1,0:T(8,128)(2,1)}, s32[2,1024]{1,0:T(2,128)S(1)}, bf16[4096,256]{1,0:T(8,128)(2,1)}, s32[]{:T(128)}) while((s32[]{:T(128)}, bf16[2,1024,256]{2,1,0:T(8,128)(2,1)}, s32[2,1024]{1,0:T(2,128)S(1)}, bf16[4096,256]{1,0:T(8,128)(2,1)}, s32[]{:T(128)}) %tuple.37), condition=%wide.region_9.10_spmd.clone, body=%wide.region_8.9_spmd.clone.sunk | while | flops 2151940096 | bytes 2634305 | solution.py:95
  105.8 5.3 %fusion.79 = bf16[2,1024,256]{2,1,0:T(8,128)(2,1)} fusion(bf16[2,1024,256]{2,1,0:T(8,128)(2,1)} %get-tuple-element.157, s32[]{:T(128)} %get-tuple-element.156, bf16[4096,256]{1,0:T(8,128)(2,1)} %get-tuple-element.164, s32[1024]{0:T(1024)S(1)} %bitcast.101), kind=kOutput, calls=%fused_computation.16.clone.1 | convolution fusion | flops 2151940096 | bytes 2626048 | tf_op jit(solution)/shard_map/while/body/eval_jaxpr/dot_general | solution.py:93
  111.0 5.3 %fusion.79 = bf16[2,1024,256]{2,1,0:T(8,128)(2,1)} fusion(bf16[2,1024,256]{2,1,0:T(8,128)(2,1)} %get-tuple-element.157, s32[]{:T(128)} %get-tuple-element.156, bf16[4096,256]{1,0:T(8,128)(2,1)} %get-tuple-element.164, s32[1024]{0:T(1024)S(1)} %bitcast.101), kind=kOutput, calls=%fused_computation.16.clone.1 | convolution fusion | flops 2151940096 | bytes 2626048 | tf_op jit(solution)/shard_map/while/body/eval_jaxpr/dot_general | solution.py:93
  116.3 18.5 %fusion.41 = bf16[2048,256]{1,0:T(8,128)(2,1)} fusion(f32[2048,256]{1,0:T(8,128)} %fusion.35, f32[2048,256]{1,0:T(8,128)} %fusion.36, f32[1,2054,256]{2,1,0:T(8,128)S(1)} %convert_element_type.94, bf16[2,1024,256]{2,1,0:T(8,128)(2,1)} %get-tuple-element.59, s32[256]{0:T(256)S(1)} %fusion.65, s32[2048]{0:T(1024)S(1)} %subtract_add_fusion), kind=kLoop, calls=%fused_computation.66 | loop fusion | flops 15728640 | bytes 8397824 | tf_op jit(solution)/shard_map/convert_element_type | solution.py:119
  134.8 18.9 %while.21 = (s32[]{:T(128)}, bf16[4,1024,256]{2,1,0:T(8,128)(2,1)}, s32[4]{0:T(128)S(1)}, s32[2048]{0:T(1024)S(1)}, bf16[2048,256]{1,0:T(8,128)(2,1)}, /*index=5*/s32[]{:T(128)}) while((s32[]{:T(128)}, bf16[4,1024,256]{2,1,0:T(8,128)(2,1)}, s32[4]{0:T(128)S(1)}, s32[2048]{0:T(1024)S(1)}, bf16[2048,256]{1,0:T(8,128)(2,1)}, ...), condition=%wide.region_11.12_spmd, body=%wide.region_10.11_spmd.sunk | while | flops 1076102144 | bytes 1589845 | solution.py:82
  136.2 3.4 %fusion.77 = bf16[4,1024,256]{2,1,0:T(8,128)(2,1)} fusion(bf16[4,1024,256]{2,1,0:T(8,128)(2,1)} %get-tuple-element.173, s32[]{:T(128)} %get-tuple-element.172, bf16[2048,256]{1,0:T(8,128)(2,1)} %get-tuple-element.182, s32[2048]{0:T(1024)S(1)} %get-tuple-element.181, s32[1024]{0:T(1024)S(1)} %iota_add_fusion.4), kind=kOutput, calls=%fused_computation.9.clone.1 | convolution fusion | flops 1076101120 | bytes 1585664 | tf_op jit(solution)/shard_map/while/body/eval_jaxpr/dot_general | solution.py:79
  140.9 3.4 %fusion.77 = bf16[4,1024,256]{2,1,0:T(8,128)(2,1)} fusion(bf16[4,1024,256]{2,1,0:T(8,128)(2,1)} %get-tuple-element.173, s32[]{:T(128)} %get-tuple-element.172, bf16[2048,256]{1,0:T(8,128)(2,1)} %get-tuple-element.182, s32[2048]{0:T(1024)S(1)} %get-tuple-element.181, s32[1024]{0:T(1024)S(1)} %iota_add_fusion.4), kind=kOutput, calls=%fused_computation.9.clone.1 | convolution fusion | flops 1076101120 | bytes 1585664 | tf_op jit(solution)/shard_map/while/body/eval_jaxpr/dot_general | solution.py:79
  145.6 3.4 %fusion.77 = bf16[4,1024,256]{2,1,0:T(8,128)(2,1)} fusion(bf16[4,1024,256]{2,1,0:T(8,128)(2,1)} %get-tuple-element.173, s32[]{:T(128)} %get-tuple-element.172, bf16[2048,256]{1,0:T(8,128)(2,1)} %get-tuple-element.182, s32[2048]{0:T(1024)S(1)} %get-tuple-element.181, s32[1024]{0:T(1024)S(1)} %iota_add_fusion.4), kind=kOutput, calls=%fused_computation.9.clone.1 | convolution fusion | flops 1076101120 | bytes 1585664 | tf_op jit(solution)/shard_map/while/body/eval_jaxpr/dot_general | solution.py:79
  150.3 3.4 %fusion.77 = bf16[4,1024,256]{2,1,0:T(8,128)(2,1)} fusion(bf16[4,1024,256]{2,1,0:T(8,128)(2,1)} %get-tuple-element.173, s32[]{:T(128)} %get-tuple-element.172, bf16[2048,256]{1,0:T(8,128)(2,1)} %get-tuple-element.182, s32[2048]{0:T(1024)S(1)} %get-tuple-element.181, s32[1024]{0:T(1024)S(1)} %iota_add_fusion.4), kind=kOutput, calls=%fused_computation.9.clone.1 | convolution fusion | flops 1076101120 | bytes 1585664 | tf_op jit(solution)/shard_map/while/body/eval_jaxpr/dot_general | solution.py:79
  153.7 9.6 %all-to-all-start.3 = ((bf16[64,64,256]{2,1,0:T(8,128)(2,1)}), bf16[64,64,256]{2,1,0:T(8,128)(2,1)S(1)}, u32[]{:S(2)}, u32[]{:S(2)}) async-start(bf16[64,64,256]{2,1,0:T(8,128)(2,1)} %bitcast.98), calls=%async_computation.3 | async-start | bytes 4194304 | tf_op jit(solution)/shard_map/all_to_all | solution.py:127
  164.6 25.8 %all-to-all-done.3 = bf16[64,64,256]{2,1,0:T(8,128)(2,1)S(1)} async-done(((bf16[64,64,256]{2,1,0:T(8,128)(2,1)}), bf16[64,64,256]{2,1,0:T(8,128)(2,1)S(1)}, u32[]{:S(2)}, u32[]{:S(2)}) %all-to-all-start.3) | async-done | bytes 2097184 | tf_op jit(solution)/shard_map/all_to_all | solution.py:127
  190.4 2.9 %log_select_fusion = f32[64,64,256]{2,1,0:T(8,128)} fusion(bf16[64,64,256]{2,1,0:T(8,128)(2,1)S(1)} %all-to-all-done.3, pred[64,64]{1,0:T(8,128)(4,1)S(1)} %iota_compare_fusion.13), kind=kLoop, calls=%fused_computation.30 | loop fusion | flops 3145728 | bytes 6295552 | tf_op jit(solution)/shard_map/jit(_where)/select_n | solution.py:132
  (54 shorter events, 16.0 us)
Async XLA Ops:
  0.0 39.2 %copy-start = (bf16[2048,256]{1,0:T(8,128)(2,1)S(1)}, bf16[2048,256]{1,0:T(8,128)(2,1)}, u32[]{:S(2)}) copy-start(bf16[2048,256]{1,0:T(8,128)(2,1)} %param.11) | copy-start | bytes 3145732
  0.0 30.8 %copy-start.2 = (bf16[1,2048,256]{2,1,0:T(8,128)(2,1)S(1)}, bf16[1,2048,256]{2,1,0:T(8,128)(2,1)}, u32[]{:S(2)}) copy-start(bf16[1,2048,256]{2,1,0:T(8,128)(2,1)} %param.10) | copy-start | bytes 3145732
  13.1 26.1 %all-to-all-start.1 = ((s32[32,1,128]{2,1,0:T(1,128)}), s32[32,1,128]{2,1,0:T(1,128)S(1)}, u32[]{:S(2)}, u32[]{:S(2)}) async-start(s32[32,1,128]{2,1,0:T(1,128)} %bitcast.20), calls=%async_computation.1 | async-start | bytes 32768 | tf_op jit(solution)/shard_map/all_to_all | solution.py:114
  22.4 8.4 %collective-permute-start = (bf16[1,3,256]{2,1,0:T(4,128)(2,1)S(1)}, bf16[1,3,256]{2,1,0:T(4,128)(2,1)S(1)}, u32[]{:S(2)}, u32[]{:S(2)}) collective-permute-start(bf16[1,3,256]{2,1,0:T(4,128)(2,1)S(1)} %get-tuple-element.92), channel_id=1, source_target_pairs={{0,1},{1,2},{2,3},{3,4},{4,5},{5,6},{6,7},{7,8},{8,9},{9,10},{10,1... | collective-permute-start | bytes 4616 | tf_op jit(solution)/shard_map/ppermute | solution.py:19
  25.9 4.8 %collective-permute-start.1 = (bf16[1,3,256]{2,1,0:T(4,128)(2,1)S(1)}, bf16[1,3,256]{2,1,0:T(4,128)(2,1)S(1)}, u32[]{:S(2)}, u32[]{:S(2)}) collective-permute-start(bf16[1,3,256]{2,1,0:T(4,128)(2,1)S(1)} %get-tuple-element.91), channel_id=1, source_target_pairs={{1,0},{2,1},{3,2},{4,3},{5,4},{6,5},{7,6},{8,7},{9,8},{10,9},{11,1... | collective-permute-start | bytes 4616 | tf_op jit(solution)/shard_map/ppermute | solution.py:21
  59.0 39.0 %all-to-all-start.2 = ((bf16[32,128,256]{2,1,0:T(8,128)(2,1)}), bf16[32,128,256]{2,1,0:T(8,128)(2,1)}, u32[]{:S(2)}, u32[]{:S(2)}) async-start(bf16[32,128,256]{2,1,0:T(8,128)(2,1)} %broadcast_select_fusion), calls=%async_computation.2 | async-start | bytes 4194304 | tf_op jit(solution)/shard_map/all_to_all | solution.py:117
  69.6 2.6 %copy-start.1 = (bf16[1,2054,256]{2,1,0:T(8,128)(2,1)S(1)}, bf16[1,2054,256]{2,1,0:T(8,128)(2,1)}, u32[]{:S(2)}) copy-start(bf16[1,2054,256]{2,1,0:T(8,128)(2,1)} %concatenate.6) | copy-start | bytes 3154948
  98.0 55.7 %all-to-all-start = ((s32[64,1,1]{2,1,0:T(1,128)}), s32[64,1,1]{2,1,0:T(1,128)S(1)}, u32[]{:S(2)}, u32[]{:S(2)}) async-start(s32[64,1,1]{2,1,0:T(1,128)} %copy.8), calls=%async_computation | async-start | bytes 65536 | tf_op jit(solution)/shard_map/all_to_all | solution.py:128
  153.7 36.7 %all-to-all-start.3 = ((bf16[64,64,256]{2,1,0:T(8,128)(2,1)}), bf16[64,64,256]{2,1,0:T(8,128)(2,1)S(1)}, u32[]{:S(2)}, u32[]{:S(2)}) async-start(bf16[64,64,256]{2,1,0:T(8,128)(2,1)} %bitcast.98), calls=%async_computation.3 | async-start | bytes 4194304 | tf_op jit(solution)/shard_map/all_to_all | solution.py:127
where the time goes:
time: 197 us; the launch traced here: 193 us
  waiting for transfers between devices  49 us (25%)
  starting transfers between devices  41.3 us (21%)
  other arithmetic  40.1 us (20%)
  local copies, waits for them, and re-layouts  36.8 us (19%)
  matrix products  25.2 us (13%)
    all_to_all x1, waiting for transfers between devices, per_device(): lax.all_to_all(outgoing, ('scene', 'shard'), split_axis=0, concat_axis=0,...  25.8 us
    all_to_all x1, waiting for transfers between devices, per_device(): lax.all_to_all(looked_up, ('orbit', 'scene'), split_axis=0, concat_axis=0...  23.2 us
    convert_element_type x1, other arithmetic, per_device(): flat = (filtered * weight.astype(jnp.float32)).astype(jnp.bfloat16)  18.5 us
    gather x1, local copies, waits for them, and re-layouts, per_device(): jnp.take(area_tiles, lax.all_to_all(request, ('orbit', 'scene'), split_ax...  16.9 us
    dot_general x4, matrix products, place_one_block(): jnp.dot(picker, values, preferred_element_type=jnp.float32)  13.4 us
    all_to_all x1, starting transfers between devices, per_device(): lax.all_to_all(looked_up, ('orbit', 'scene'), split_axis=0, concat_axis=0...  10.5 us
    dot_general x2, matrix products, pick_one_block(): jnp.dot(picker, table, preferred_element_type=jnp.float32)  10.5 us
    all_to_all x1, starting transfers between devices, per_device(): lax.all_to_all(outgoing, ('scene', 'shard'), split_axis=0, concat_axis=0,...  9.61 us
  transfers between devices with their start and end apart: 6, of which 2 were waited for; matrix products, arithmetic and copies ran while one was open for 34% of the time, Pallas kernels for 0%

commit v1 on v0

v1 whole, which is shorter than its diff:
```python
import jax
import jax.numpy as jnp
from jax import lax
from jax.experimental import pallas as pl
from jax.experimental.pallas import tpu as pltpu
from jax.sharding import PartitionSpec as P

NOISE = 0.25
ROWS = 2048
PIX = 256
OWNERS = 32
CAPT = 128
TRAINERS = 64
CAPR = 64
RG = 4
TG = 8
HALO = 16
LEE = 64
MESH = pl.DeviceIdType.MESH
F32, BF16 = jnp.float32, jnp.bfloat16
PLANE_STRIDE = 11
CUBE_STRIDE = 23


def iota(shape, dim):
    return lax.broadcasted_iota(jnp.int32, shape, dim).astype(F32)


def dot(a, b):
    return jnp.dot(a, b, preferred_element_type=F32)


def mask(hit):
    return jnp.where(hit, 1.0, 0.0).astype(BF16)


def body(
    sigma, area, owner, slot, band, seam, out,
    sum1, sum2, filtered, weight, flat, source, source_row, target_row,
    ask_out, ask_in, rep_out, rep_in, put_out, put_in, halo_in,
    halo_send, halo_recv, ask_send, ask_recv, rep_send, rep_recv, put_send, put_recv,
):
    orbit, scene, shard = (lax.axis_index(name) for name in ("orbit", "scene", "shard"))
    y, x = scene // 4, scene % 4
    block = scene * 4 + shard

    def plane(k, sign):
        step = (k * PLANE_STRIDE) % OWNERS
        dy, dx = sign * (step // 8) + 4, sign * ((step // 2) % 4) + 4
        return ((orbit + step % 2) % 2, ((y + dy) % 4) * 4 + (x + dx) % 4, shard)

    def cube(k, sign):
        step = (k * CUBE_STRIDE) % TRAINERS
        dy, dx, dz = (sign * d + 4 for d in (step // 16, (step // 4) % 4, step % 4))
        return (orbit, ((y + dy) % 4) * 4 + (x + dx) % 4, (shard + dz) % 4)

    def owner_of(device):
        return device[0] * 16 + device[1]

    def trainer_of(device):
        return device[1] * 4 + device[2]

    barrier = pltpu.get_barrier_semaphore()

    def greet_other(k, carry):
        pl.semaphore_signal(barrier, inc=1, device_id=((orbit + 1) % 2, k, shard), device_id_type=MESH)
        return carry

    def greet_own(k, carry):
        pl.semaphore_signal(barrier, inc=1, device_id=cube(k, 1), device_id_type=MESH)
        return carry

    lax.fori_loop(0, 16, greet_other, 0)
    lax.fori_loop(1, TRAINERS, greet_own, 0)

    upper = mask(iota((256, 256), 0) < iota((256, 256), 1))
    seen = jnp.zeros((OWNERS + TRAINERS, 1), F32)
    wanted = jnp.zeros((2 * OWNERS, CAPT), F32)
    for part in range(ROWS // 256):
        lanes = pl.ds(part * 256, 256)
        own = owner[:, lanes].astype(F32)
        trainer = ((band[:, lanes] + seam[...]) & (TRAINERS - 1)).astype(F32)
        own_hot = jnp.where(iota((OWNERS, 256), 0) == own, 1.0, 0.0)
        trainer_hot = jnp.where(iota((TRAINERS, 256), 0) == trainer, 1.0, 0.0)
        hot = jnp.concatenate([own_hot, trainer_hot], axis=0)
        before = (dot(hot.astype(BF16), upper) + seen) * hot
        seen = seen + jnp.sum(hot, axis=1, keepdims=True)
        order_in = jnp.sum(before[:OWNERS], axis=0, keepdims=True)
        order_out = jnp.sum(before[OWNERS:], axis=0, keepdims=True)
        source_row[:, lanes] = own * CAPT + order_in
        target_row[:, lanes] = trainer * CAPR + order_out
        place = slot[:, lanes]
        high, low = (place >> 8).astype(F32), (place & 255).astype(F32)
        parts = jnp.concatenate([own_hot * high, own_hot * low], axis=0).astype(BF16)
        wanted = wanted + lax.dot_general(
            parts, mask(iota((CAPT, 256), 0) == order_in),
            (((1,), (1,)), ((), ())), preferred_element_type=F32,
        )
    positions = (wanted[:OWNERS] * 256.0 + wanted[OWNERS:]).astype(jnp.int32)
    for index in range(OWNERS):
        ask_out[index] = positions[index : index + 1, :]

    pl.semaphore_wait(barrier, 16 + TRAINERS - 1)

    pltpu.make_async_copy(ask_out.at[owner_of((orbit, scene))], ask_in.at[0], ask_recv.at[0]).start()

    def send_ask(k, carry):
        peer = plane(k, 1)
        pltpu.make_async_remote_copy(
            ask_out.at[owner_of(peer)], ask_in.at[k], ask_send, ask_recv.at[k // RG],
            device_id=peer, device_id_type=MESH,
        ).start()
        return carry

    lax.fori_loop(1, OWNERS, send_ask, 0)

    def halo_copy(side):
        peer = block + 1 - 2 * side
        rows = pl.ds((1 - side) * (ROWS - HALO), HALO)
        return pltpu.make_async_remote_copy(
            sigma.at[rows], halo_in.at[side], halo_send.at[side], halo_recv.at[side],
            device_id=(orbit, peer // 4, peer % 4), device_id_type=MESH,
        )

    has_side = (block > 0, block < TRAINERS - 1)
    for side in range(2):

        @pl.when(has_side[1 - side])
        def _():
            halo_copy(side).start()

        @pl.when(jnp.logical_not(has_side[side]))
        def _():
            halo_in[side] = jnp.zeros((HALO, PIX), BF16)

    near = mask(jnp.abs(iota((PIX, PIX), 0) - iota((PIX, PIX), 1)) < 4.0)

    def row_sums(cells, rows):
        wide = cells.astype(F32)
        square = wide * wide
        high = square.astype(BF16)
        low = (square - high.astype(F32)).astype(BF16)
        sum1[rows] = dot(cells, near)
        sum2[rows] = dot(high, near) + dot(low, near)

    def sums_step(part, carry):
        row_sums(sigma[pl.ds(pl.multiple_of(part * 256, 256), 256)], pl.ds(pl.multiple_of(part * 256 + HALO, HALO), 256))
        return carry

    lax.fori_loop(0, ROWS // 256, sums_step, 0)

    for part in range(ROWS // 128):
        row = source_row[:, pl.ds(part * 128, 128)]
        source[pl.ds(part * 128, 128)] = jnp.transpose(jnp.broadcast_to(row, (128, 128)))

    def gather_step(step, carry):
        group = pl.ds(step * RG, RG)
        pltpu.make_async_copy(ask_in.at[group], ask_in.at[group], ask_recv.at[step]).wait()
        columns = [
            jnp.transpose(jnp.broadcast_to(ask_in[step * RG + j].astype(F32), (CAPT, CAPT)))
            for j in range(RG)
        ]
        column = jnp.concatenate(columns, axis=0)
        lane = iota((RG * CAPT, 128), 1)
        picker = jnp.concatenate([mask(column == lane + 128.0 * c) for c in range(ROWS // 128)], axis=1)
        rep_out[group] = dot(picker, area[...]).astype(BF16).reshape(RG, CAPT, PIX)
        for j in range(RG):
            k = step * RG + j

            @pl.when(k == 0)
            def _():
                pltpu.make_async_copy(rep_out.at[k], rep_in.at[k], rep_recv.at[step]).start()

            @pl.when(k > 0)
            def _():
                pltpu.make_async_remote_copy(
                    rep_out.at[k], rep_in.at[k], rep_send, rep_recv.at[step],
                    device_id=plane(k, -1), device_id_type=MESH,
                ).start()

        return carry

    lax.fori_loop(0, OWNERS // RG, gather_step, 0)

    for side in range(2):

        @pl.when(has_side[side])
        def _():
            halo_copy(side).wait_recv()

        row_sums(halo_in[side], pl.ds(side * (ROWS + HALO), HALO))

    pixel = iota((LEE, PIX), 1)
    col_span = jnp.minimum(pixel + 3.0, PIX - 1.0) - jnp.maximum(pixel - 3.0, 0.0) + 1.0
    line = iota((LEE, PIX), 0)

    def seven(cells):
        rows = cells.shape[0]
        two = cells + pltpu.roll(cells, rows - 1, 0)
        four = two + pltpu.roll(two, rows - 2, 0)
        total = four + pltpu.roll(two, rows - 4, 0) + pltpu.roll(cells, rows - 6, 0)
        return pltpu.roll(total, rows - 5, 0)[:LEE]

    def lee_step(part, carry):
        start = pl.multiple_of(part * LEE, LEE)
        slab = pl.ds(pl.multiple_of(start + 8, 8), LEE + 16)
        at = line + (block * ROWS + start).astype(F32)
        row_span = jnp.minimum(at + 3.0, TRAINERS * ROWS - 1.0) - jnp.maximum(at - 3.0, 0.0) + 1.0
        share = 1.0 / (row_span * col_span)
        center = sigma[pl.ds(start, LEE)].astype(F32)
        mean = seven(sum1[slab]) * share
        power = mean * mean
        variance = seven(sum2[slab]) * share - power
        speckle = NOISE * power
        mixing = jnp.maximum(variance - speckle, 0.0) / (variance + speckle)
        filtered[pl.ds(start, LEE)] = mean + mixing * (center - mean)
        return carry

    lax.fori_loop(0, ROWS // LEE, lee_step, 0)

    def pick_step(step, carry):
        group = pl.ds(step * RG, RG)
        pltpu.make_async_copy(rep_in.at[group], rep_in.at[group], rep_recv.at[step]).wait()
        table = rep_in[group].reshape(RG * CAPT, PIX)
        firsts = [(owner_of(plane(step * RG + j, 1)) * CAPT).astype(F32) for j in range(RG)]
        lane = iota((512, CAPT), 1)

        def rows_step(part, inner):
            rows = pl.ds(pl.multiple_of(part * 512, 512), 512)
            column = source[rows]
            picker = jnp.concatenate([mask(column == lane + first) for first in firsts], axis=1)
            picked = dot(picker, table)
            weight[rows] = jnp.where(step > 0, weight[rows] + picked, picked)
            return inner

        return lax.fori_loop(0, ROWS // 512, rows_step, carry)

    weight[...] = jnp.zeros((ROWS, PIX), F32)
    lax.fori_loop(0, OWNERS // RG, pick_step, 0)
    flat[...] = (filtered[...] * weight[...]).astype(BF16)

    def place_step(step, carry):
        group = pl.ds(step * TG, TG)
        row = target_row[...]
        line = iota((CAPR, ROWS), 0)
        pickers = []
        for j in range(TG):
            first = (trainer_of(cube(step * TG + j, 1)) * CAPR).astype(F32)
            pickers.append(mask(line == row - first))
        placed = dot(jnp.concatenate(pickers, axis=0), flat[...])
        put_out[group] = placed.astype(BF16).reshape(TG, CAPR, PIX)
        for j in range(TG):
            k = step * TG + j

            @pl.when(k == 0)
            def _():
                pltpu.make_async_copy(put_out.at[k], put_in.at[k], put_recv.at[step]).start()

            @pl.when(k > 0)
            def _():
                pltpu.make_async_remote_copy(
                    put_out.at[k], put_in.at[k], put_send, put_recv.at[step],
                    device_id=cube(k, 1), device_id_type=MESH,
                ).start()

        return carry

    lax.fori_loop(0, TRAINERS // TG, place_step, 0)

    def log_step(step, carry):
        group = pl.ds(step * TG, TG)
        pltpu.make_async_copy(put_in.at[group], put_in.at[group], put_recv.at[step]).wait()

        def one(j, inner):
            k = step * TG + j
            values = put_in[k].astype(F32)
            filled = values > 0.0
            logs = jnp.where(filled, jnp.log(jnp.where(filled, values, 1.0)), 0.0)
            first = pl.multiple_of(trainer_of(cube(k, -1)) * CAPR, CAPR)
            out[pl.ds(first, CAPR)] = logs
            return inner

        return lax.fori_loop(0, TG, one, carry)

    lax.fori_loop(0, TRAINERS // TG, log_step, 0)

    for buffer, sem, count in (
        (ask_out, ask_send, OWNERS - 1),
        (rep_out, rep_send, OWNERS - 1),
        (put_out, put_send, TRAINERS - 1),
    ):
        part = buffer.at[pl.ds(1, count)]
        pltpu.make_async_copy(part, part, sem).wait()
    for side in range(2):

        @pl.when(has_side[1 - side])
        def _():
            halo_copy(side).wait_send()


def per_device(sigma0, area_tiles, tile_owner, tile_slot, trainer_band, seam_offset):
    vmem = pl.BlockSpec(memory_space=pltpu.VMEM)
    dma = pltpu.SemaphoreType.DMA
    patches = pl.pallas_call(
        body,
        out_shape=jax.ShapeDtypeStruct((TRAINERS * CAPR, PIX), F32),
        in_specs=[vmem] * 6,
        out_specs=vmem,
        scratch_shapes=[
            pltpu.VMEM((ROWS + 2 * HALO, PIX), F32),
            pltpu.VMEM((ROWS + 2 * HALO, PIX), F32),
            pltpu.VMEM((ROWS, PIX), F32),
            pltpu.VMEM((ROWS, PIX), F32),
            pltpu.VMEM((ROWS, PIX), BF16),
            pltpu.VMEM((ROWS, 128), F32),
            pltpu.VMEM((1, ROWS), F32),
            pltpu.VMEM((1, ROWS), F32),
            pltpu.VMEM((OWNERS, 1, CAPT), jnp.int32),
            pltpu.VMEM((OWNERS, 1, CAPT), jnp.int32),
            pltpu.VMEM((OWNERS, CAPT, PIX), BF16),
            pltpu.VMEM((OWNERS, CAPT, PIX), BF16),
            pltpu.VMEM((TRAINERS, CAPR, PIX), BF16),
            pltpu.VMEM((TRAINERS, CAPR, PIX), BF16),
            pltpu.VMEM((2, HALO, PIX), BF16),
            dma((2,)),
            dma((2,)),
            dma(()),
            dma((OWNERS // RG,)),
            dma(()),
            dma((OWNERS // RG,)),
            dma(()),
            dma((TRAINERS // TG,)),
        ],
        compiler_params=pltpu.CompilerParams(
            collective_id=0, has_side_effects=True, vmem_limit_bytes=50 << 20
        ),
        cost_estimate=pl.CostEstimate(flops=16 << 30, bytes_accessed=8 << 20, transcendentals=1 << 20),
    )(
        sigma0[0],
        area_tiles,
        tile_owner.reshape(1, ROWS),
        tile_slot,
        trainer_band.reshape(1, ROWS),
        seam_offset,
    )
    return patches[None]


def solution(mesh):
    return jax.shard_map(
        per_device,
        mesh=mesh,
        in_specs=(
            P("orbit", ("scene", "shard"), None),
            P(("orbit", "scene"), None),
            P("orbit", ("scene", "shard"), None),
            P("orbit", ("scene", "shard")),
            P("orbit", ("scene", "shard"), None),
            P("orbit", ("scene", "shard")),
        ),
        out_specs=P("orbit", ("scene", "shard"), None),
        check_vma=False,
    )
```

time: 197 us -> 85.3 us (0.43); the launches traced: 193 us -> 84.9 us
  Pallas kernels: 0 us -> 75.2 us
  waiting for transfers between devices: 49 us -> 0 us
  starting transfers between devices: 41.3 us -> 0 us
  other arithmetic: 40.1 us -> 0 us
  local copies, waits for them, and re-layouts: 36.8 us -> 9 us
  matrix products: 25.2 us -> 0 us
    pallas_call x0 -> x1, Pallas kernels: none -> 75.2 us  [per_device(): pl.pallas_call(body, out_shape=jax.ShapeDtypeStruct((TRAINERS * CAPR, PIX...]
    all_to_all x4 -> x0, waiting for transfers between devices: 49 us -> none  [the longest x1 25.8 us: per_device(): lax.all_to_all(outgoing, ('scene', 'shard'), split_axis=0, concat_axis=0,...]
    all_to_all x4 -> x0, starting transfers between devices: 36.5 us -> none  [the longest x1 10.5 us: per_device(): lax.all_to_all(looked_up, ('orbit', 'scene'), split_axis=0, concat_axis=0...]
    dot_general x8 -> x0, matrix products: 25.2 us -> none  [the longest x4 13.4 us: place_one_block(): jnp.dot(picker, values, preferred_element_type=jnp.float32)]
    convert_element_type x4 -> x0, other arithmetic: 19.8 us -> none  [the longest x1 18.5 us: per_device(): flat = (filtered * weight.astype(jnp.float32)).astype(jnp.bfloat16)]
    gather x1 -> x0, local copies, waits for them, and re-layouts: 16.9 us -> none  [per_device(): jnp.take(area_tiles, lax.all_to_all(request, ('orbit', 'scene'), split_ax...]
    add x11 -> x0, other arithmetic: 8.58 us -> none  [the longest x2 5.08 us: window_sum(): vertical = vertical + padded[offset:offset + count_rows]]
    concatenate x1 -> x0, local copies, waits for them, and re-layouts: 6.95 us -> none  [with_halo(): jnp.concatenate([lax.ppermute(tail, axis, [(i, (i + 1) % count) for i in...]
  transfers between devices with their start and end apart: 6 -> 0, of which waited for: 2 -> 0; matrix products, arithmetic and copies ran while one was open for 34% -> 0% of each run, Pallas kernels for 0% -> 0%
where the time goes in v1:
time: 85.3 us; the launch traced here: 84.9 us
  Pallas kernels  75.2 us (88%)
  local copies, waits for them, and re-layouts  9 us (11%)
    pallas_call x1, Pallas kernels, per_device(): pl.pallas_call(body, out_shape=jax.ShapeDtypeStruct((TRAINERS * CAPR, PIX...  75.2 us
    unnamed x11, local copies, waits for them, and re-layouts  9 us

profile of v1, /device:TPU:1, one launch (start us, length us, event | category | flops | bytes accessed | tf_op | source)
XLA Modules:
  0.0 84.9 jit_solution(5489588305076980361)
XLA Ops:
  0.7 0.0 copy-start
  0.7 1.2 %copy-done = bf16[1,2048,256]{2,1,0:T(8,128)(2,1)S(1)} copy-done((bf16[1,2048,256]{2,1,0:T(8,128)(2,1)S(1)}, bf16[1,2048,256]{2,1,0:T(8,128)(2,1)}, u32[]{:S(2)}) %copy-start) | copy-done | bytes 1048600
  1.9 0.0 copy-start.1
  1.9 1.2 %copy-done.1 = bf16[2048,256]{1,0:T(8,128)(2,1)S(1)} copy-done((bf16[2048,256]{1,0:T(8,128)(2,1)S(1)}, bf16[2048,256]{1,0:T(8,128)(2,1)}, u32[]{:S(2)}) %copy-start.1) | copy-done | bytes 1048600
  3.1 0.0 copy-start.2
  3.1 0.7 copy-done.2
  3.8 0.0 copy-start.3
  3.8 0.7 copy-done.3
  4.5 0.0 copy-start.4
  4.5 0.7 copy-done.4
  5.2 75.2 %shard_map.64 = f32[4096,256]{1,0:T(8,128)} custom-call(bf16[2048,256]{1,0:T(8,128)(2,1)S(1)} %bitcast.4, bf16[2048,256]{1,0:T(8,128)(2,1)S(1)} %copy-done.1, s32[1,2048]{1,0:T(1,128)S(1)} %bitcast.5, s32[1,2048]{1,0:T(1,128)S(1)} %copy-done.3, s32[1,2048]{1,0:T(1,128)S(1)} %bitcast.6, s32[1,1]{1,0:T(1,128)S(6)} %copy.8.seam), custom_call_target="tpu_custom_call" | custom-call | flops 17179869184 | bytes 8388608 | tf_op jit(solution)/shard_map/pallas_call | solution.py:304
  80.4 4.5 %copy.9 = f32[1,4096,256]{2,1,0:T(8,128)} copy(f32[1,4096,256]{2,1,0:T(8,128)} %bitcast.7) | data formatting | bytes 8388608
Async XLA Ops:
  0.7 1.2 %copy-start = (bf16[1,2048,256]{2,1,0:T(8,128)(2,1)S(1)}, bf16[1,2048,256]{2,1,0:T(8,128)(2,1)}, u32[]{:S(2)}) copy-start(bf16[1,2048,256]{2,1,0:T(8,128)(2,1)} %param.6) | copy-start | bytes 3145732
  1.9 1.2 %copy-start.1 = (bf16[2048,256]{1,0:T(8,128)(2,1)S(1)}, bf16[2048,256]{1,0:T(8,128)(2,1)}, u32[]{:S(2)}) copy-start(bf16[2048,256]{1,0:T(8,128)(2,1)} %area.1) | copy-start | bytes 3145732
  3.1 0.7 copy-start.2
  3.8 0.7 copy-start.3
  4.5 0.7 copy-start.4

commit v2 on v1

--- a/solution.py
+++ b/solution.py
@@ -35,10 +35,10 @@
 
 
 def body(
-    sigma, area, owner, slot, band, seam, out,
-    sum1, sum2, filtered, weight, flat, source, source_row, target_row,
-    ask_out, ask_in, rep_out, rep_in, put_out, put_in, halo_in,
-    halo_send, halo_recv, ask_send, ask_recv, rep_send, rep_recv, put_send, put_recv,
+    sigma_hbm, area_hbm, owner_hbm, slot_hbm, band_hbm, seam, put_in,
+    sigma, area, owner, slot, band, loaded, sum1, sum2, filtered, weight, flat, source, source_row, target_row,
+    ask_out, ask_in, rep_out, rep_in, put_out, halo_in,
+    halo_send, halo_recv, ask_send, ask_recv, rep_send, rep_recv, put_send, put_recv, planes,
 ):
     orbit, scene, shard = (lax.axis_index(name) for name in ("orbit", "scene", "shard"))
     y, x = scene // 4, scene % 4
@@ -60,18 +60,34 @@
     def trainer_of(device):
         return device[1] * 4 + device[2]
 
+    loads = [
+        pltpu.make_async_copy(*ends, loaded.at[index])
+        for index, ends in enumerate(
+            ((owner_hbm, owner), (slot_hbm, slot), (band_hbm, band), (sigma_hbm, sigma), (area_hbm, area))
+        )
+    ]
+    for load in loads:
+        load.start()
+
     barrier = pltpu.get_barrier_semaphore()
 
-    def greet_other(k, carry):
-        pl.semaphore_signal(barrier, inc=1, device_id=((orbit + 1) % 2, k, shard), device_id_type=MESH)
-        return carry
-
-    def greet_own(k, carry):
-        pl.semaphore_signal(barrier, inc=1, device_id=cube(k, 1), device_id_type=MESH)
-        return carry
-
-    lax.fori_loop(0, 16, greet_other, 0)
-    lax.fori_loop(1, TRAINERS, greet_own, 0)
+    def greet(device):
+        pl.semaphore_signal(barrier, inc=1, device_id=device, device_id_type=MESH)
+
+    def greet_plane(k, carry):
+        greet(plane(k, 1))
+        return carry
+
+    lax.fori_loop(1, OWNERS, greet_plane, 0)
+    column = [(orbit, scene, (shard + d) % 4) for d in range(1, 4)]
+    for device in column:
+        greet(device)
+    for side in (1, TRAINERS - 1):
+        peer = (block + side) % TRAINERS
+        greet((orbit, peer // 4, peer % 4))
+
+    for load in loads[:3]:
+        load.wait()
 
     upper = mask(iota((256, 256), 0) < iota((256, 256), 1))
     seen = jnp.zeros((OWNERS + TRAINERS, 1), F32)
@@ -100,7 +116,7 @@
     for index in range(OWNERS):
         ask_out[index] = positions[index : index + 1, :]
 
-    pl.semaphore_wait(barrier, 16 + TRAINERS - 1)
+    pl.semaphore_wait(barrier, OWNERS - 1 + 3 + 2)
 
     pltpu.make_async_copy(ask_out.at[owner_of((orbit, scene))], ask_in.at[0], ask_recv.at[0]).start()
 
@@ -122,6 +138,7 @@
             device_id=(orbit, peer // 4, peer % 4), device_id_type=MESH,
         )
 
+    loads[3].wait()
     has_side = (block > 0, block < TRAINERS - 1)
     for side in range(2):
 
@@ -152,6 +169,8 @@
     for part in range(ROWS // 128):
         row = source_row[:, pl.ds(part * 128, 128)]
         source[pl.ds(part * 128, 128)] = jnp.transpose(jnp.broadcast_to(row, (128, 128)))
+
+    loads[4].wait()
 
     def gather_step(step, carry):
         group = pl.ds(step * RG, RG)
@@ -182,6 +201,9 @@
 
     lax.fori_loop(0, OWNERS // RG, gather_step, 0)
 
+    for device in column:
+        pl.semaphore_signal(planes, inc=1, device_id=device, device_id_type=MESH)
+
     for side in range(2):
 
         @pl.when(has_side[side])
@@ -237,6 +259,7 @@
 
     weight[...] = jnp.zeros((ROWS, PIX), F32)
     lax.fori_loop(0, OWNERS // RG, pick_step, 0)
+    pl.semaphore_wait(planes, 3)
     flat[...] = (filtered[...] * weight[...]).astype(BF16)
 
     def place_step(step, carry):
@@ -254,12 +277,12 @@
 
             @pl.when(k == 0)
             def _():
-                pltpu.make_async_copy(put_out.at[k], put_in.at[k], put_recv.at[step]).start()
+                pltpu.make_async_copy(put_out.at[k], put_in.at[block], put_recv.at[0]).start()
 
             @pl.when(k > 0)
             def _():
                 pltpu.make_async_remote_copy(
-                    put_out.at[k], put_in.at[k], put_send, put_recv.at[step],
+                    put_out.at[k], put_in.at[block], put_send, put_recv.at[0],
                     device_id=cube(k, 1), device_id_type=MESH,
                 ).start()
 
@@ -267,22 +290,7 @@
 
     lax.fori_loop(0, TRAINERS // TG, place_step, 0)
 
-    def log_step(step, carry):
-        group = pl.ds(step * TG, TG)
-        pltpu.make_async_copy(put_in.at[group], put_in.at[group], put_recv.at[step]).wait()
-
-        def one(j, inner):
-            k = step * TG + j
-            values = put_in[k].astype(F32)
-            filled = values > 0.0
-            logs = jnp.where(filled, jnp.log(jnp.where(filled, values, 1.0)), 0.0)
-            first = pl.multiple_of(trainer_of(cube(k, -1)) * CAPR, CAPR)
-            out[pl.ds(first, CAPR)] = logs
-            return inner
-
-        return lax.fori_loop(0, TG, one, carry)
-
-    lax.fori_loop(0, TRAINERS // TG, log_step, 0)
+    pltpu.make_async_copy(put_in, put_in, put_recv.at[0]).wait()
 
     for buffer, sem, count in (
         (ask_out, ask_send, OWNERS - 1),
@@ -298,15 +306,35 @@
             halo_copy(side).wait_send()
 
 
+def log_body(values, patches, logs, sems):
+    copies = []
+    for step in range(TRAINERS // TG):
+        rows = pl.ds(step * TG * CAPR, TG * CAPR)
+        value = values[pl.ds(step * TG, TG)].reshape(TG * CAPR, PIX).astype(F32)
+        filled = value > 0.0
+        logs[rows] = jnp.where(filled, jnp.log(jnp.where(filled, value, 1.0)), 0.0)
+        copies.append(pltpu.make_async_copy(logs.at[rows], patches.at[rows], sems.at[step]))
+        copies[-1].start()
+    for copy in copies:
+        copy.wait()
+
+
 def per_device(sigma0, area_tiles, tile_owner, tile_slot, trainer_band, seam_offset):
     vmem = pl.BlockSpec(memory_space=pltpu.VMEM)
     dma = pltpu.SemaphoreType.DMA
-    patches = pl.pallas_call(
+    hbm = pl.BlockSpec(memory_space=pltpu.HBM)
+    arrived = pl.pallas_call(
         body,
-        out_shape=jax.ShapeDtypeStruct((TRAINERS * CAPR, PIX), F32),
-        in_specs=[vmem] * 6,
+        out_shape=jax.ShapeDtypeStruct((TRAINERS, CAPR, PIX), BF16),
+        in_specs=[hbm] * 5 + [vmem],
         out_specs=vmem,
         scratch_shapes=[
+            pltpu.VMEM((ROWS, PIX), BF16),
+            pltpu.VMEM((ROWS, PIX), BF16),
+            pltpu.VMEM((1, ROWS), jnp.int32),
+            pltpu.VMEM((1, ROWS), jnp.int32),
+            pltpu.VMEM((1, ROWS), jnp.int32),
+            dma((5,)),
             pltpu.VMEM((ROWS + 2 * HALO, PIX), F32),
             pltpu.VMEM((ROWS + 2 * HALO, PIX), F32),
             pltpu.VMEM((ROWS, PIX), F32),
@@ -320,7 +348,6 @@
             pltpu.VMEM((OWNERS, CAPT, PIX), BF16),
             pltpu.VMEM((OWNERS, CAPT, PIX), BF16),
             pltpu.VMEM((TRAINERS, CAPR, PIX), BF16),
-            pltpu.VMEM((TRAINERS, CAPR, PIX), BF16),
             pltpu.VMEM((2, HALO, PIX), BF16),
             dma((2,)),
             dma((2,)),
@@ -329,20 +356,34 @@
             dma(()),
             dma((OWNERS // RG,)),
             dma(()),
-            dma((TRAINERS // TG,)),
+            dma((1,)),
+            pltpu.SemaphoreType.REGULAR,
         ],
         compiler_params=pltpu.CompilerParams(
-            collective_id=0, has_side_effects=True, vmem_limit_bytes=50 << 20
+            collective_id=0, has_side_effects=True, vmem_limit_bytes=36 << 20
         ),
         cost_estimate=pl.CostEstimate(flops=16 << 30, bytes_accessed=8 << 20, transcendentals=1 << 20),
     )(
-        sigma0[0],
-        area_tiles,
-        tile_owner.reshape(1, ROWS),
-        tile_slot,
-        trainer_band.reshape(1, ROWS),
+        *(
+            pltpu.with_memory_space_constraint(array, pltpu.HBM)
+            for array in (
+                sigma0[0],
+                area_tiles,
+                tile_owner.reshape(1, ROWS),
+                tile_slot,
+                trainer_band.reshape(1, ROWS),
+            )
+        ),
         seam_offset,
     )
+    patches = pl.pallas_call(
+        log_body,
+        out_shape=jax.ShapeDtypeStruct((TRAINERS * CAPR, PIX), F32),
+        in_specs=[vmem],
+        out_specs=hbm,
+        scratch_shapes=[pltpu.VMEM((TRAINERS * CAPR, PIX), F32), dma((TRAINERS // TG,))],
+        compiler_params=pltpu.CompilerParams(vmem_limit_bytes=16 << 20),
+    )(arrived)
     return patches[None]
 
 

time: 85.3 us -> 74.2 us (0.87)
  local copies, waits for them, and re-layouts: 9 us -> 0 us
  Pallas kernels: 75.2 us -> 73.4 us
    unnamed x11 -> x0, local copies, waits for them, and re-layouts: 9 us -> none
    pallas_call x1 -> x2, Pallas kernels: 75.2 us -> 73.4 us  [the longest x1 71.3 us: per_device(): pl.pallas_call(body, out_shape=jax.ShapeDtypeStruct((TRAINERS, CAPR, PIX)...]
where the time goes in v2:
time: 74.2 us; the launch traced here: 74.1 us
  Pallas kernels  73.4 us (99%)
    pallas_call x1, Pallas kernels, per_device(): pl.pallas_call(body, out_shape=jax.ShapeDtypeStruct((TRAINERS, CAPR, PIX)...  71.3 us
    pallas_call x1, Pallas kernels, per_device(): pl.pallas_call(log_body, out_shape=jax.ShapeDtypeStruct((TRAINERS * CAPR,...  2.18 us

profile of v2, /device:TPU:1, one launch (start us, length us, event | category | flops | bytes accessed | tf_op | source)
XLA Modules:
  0.0 74.1 jit_solution(11184053249211045111)
XLA Ops:
  0.7 71.3 %shard_map.64.values = bf16[64,64,256]{2,1,0:T(8,128)(2,1)S(1)} custom-call(bf16[2048,256]{1,0:T(8,128)(2,1)} %bitcast.4, bf16[2048,256]{1,0:T(8,128)(2,1)} %area_hbm.1, s32[1,2048]{1,0:T(1,128)} %bitcast.5, s32[1,2048]{1,0:T(1,128)} %slot_hbm.1, s32[1,2048]{1,0:T(1,128)} %bitcast.6, s32[1,1]{1,0:T(1,128)S(6)} %copy.7.seam), custom_call_target="tpu_custom_call" | custom-call | flops 17179869184 | bytes 8388608 | tf_op jit(solution)/shard_map/pallas_call | solution.py:326
  71.9 2.2 %shard_map.65 = f32[4096,256]{1,0:T(8,128)} custom-call(bf16[64,64,256]{2,1,0:T(8,128)(2,1)S(1)} %shard_map.64.values), custom_call_target="tpu_custom_call" | custom-call | tf_op jit(solution)/shard_map/pallas_call | solution.py:379

commit v3 on v2

--- a/solution.py
+++ b/solution.py
@@ -1,3 +1,5 @@
+import functools
+
 import jax
 import jax.numpy as jnp
 from jax import lax
@@ -13,12 +15,15 @@
 TRAINERS = 64
 CAPR = 64
 RG = 4
-TG = 8
+PG = (8, 4)
+TG = (16, 8)
+LOG = 8
 HALO = 16
+HALF = PIX // 2
 LEE = 64
 MESH = pl.DeviceIdType.MESH
 F32, BF16 = jnp.float32, jnp.bfloat16
-PLANE_STRIDE = 11
+PLANE_STRIDE = 27
 CUBE_STRIDE = 23
 
 
@@ -28,6 +33,14 @@
 
 def dot(a, b):
     return jnp.dot(a, b, preferred_element_type=F32)
+
+
+def rem(a, b):
+    return lax.rem(a, jnp.int32(b))
+
+
+def div(a, b):
+    return lax.div(a, jnp.int32(b))
 
 
 def mask(hit):
@@ -41,18 +54,18 @@
     halo_send, halo_recv, ask_send, ask_recv, rep_send, rep_recv, put_send, put_recv, planes,
 ):
     orbit, scene, shard = (lax.axis_index(name) for name in ("orbit", "scene", "shard"))
-    y, x = scene // 4, scene % 4
+    y, x = div(scene, 4), rem(scene, 4)
     block = scene * 4 + shard
 
     def plane(k, sign):
-        step = (k * PLANE_STRIDE) % OWNERS
-        dy, dx = sign * (step // 8) + 4, sign * ((step // 2) % 4) + 4
-        return ((orbit + step % 2) % 2, ((y + dy) % 4) * 4 + (x + dx) % 4, shard)
+        step = rem(k * PLANE_STRIDE, OWNERS)
+        dy, dx = sign * div(step, 8) + 4, sign * rem(div(step, 2), 4) + 4
+        return (rem(orbit + rem(step, 2), 2), rem(y + dy, 4) * 4 + rem(x + dx, 4), shard)
 
     def cube(k, sign):
-        step = (k * CUBE_STRIDE) % TRAINERS
-        dy, dx, dz = (sign * d + 4 for d in (step // 16, (step // 4) % 4, step % 4))
-        return (orbit, ((y + dy) % 4) * 4 + (x + dx) % 4, (shard + dz) % 4)
+        step = rem(k * CUBE_STRIDE, TRAINERS)
+        dy, dx, dz = (sign * d + 4 for d in (div(step, 16), rem(div(step, 4), 4), rem(step, 4)))
+        return (orbit, rem(y + dy, 4) * 4 + rem(x + dx, 4), rem(shard + dz, 4))
 
     def owner_of(device):
         return device[0] * 16 + device[1]
@@ -79,12 +92,12 @@
         return carry
 
     lax.fori_loop(1, OWNERS, greet_plane, 0)
-    column = [(orbit, scene, (shard + d) % 4) for d in range(1, 4)]
+    column = [(orbit, scene, rem(shard + d, 4)) for d in range(1, 4)]
     for device in column:
         greet(device)
     for side in (1, TRAINERS - 1):
-        peer = (block + side) % TRAINERS
-        greet((orbit, peer // 4, peer % 4))
+        peer = rem(block + side, TRAINERS)
+        greet((orbit, div(peer, 4), rem(peer, 4)))
 
     for load in loads[:3]:
         load.wait()
@@ -116,39 +129,7 @@
     for index in range(OWNERS):
         ask_out[index] = positions[index : index + 1, :]
 
-    pl.semaphore_wait(barrier, OWNERS - 1 + 3 + 2)
-
-    pltpu.make_async_copy(ask_out.at[owner_of((orbit, scene))], ask_in.at[0], ask_recv.at[0]).start()
-
-    def send_ask(k, carry):
-        peer = plane(k, 1)
-        pltpu.make_async_remote_copy(
-            ask_out.at[owner_of(peer)], ask_in.at[k], ask_send, ask_recv.at[k // RG],
-            device_id=peer, device_id_type=MESH,
-        ).start()
-        return carry
-
-    lax.fori_loop(1, OWNERS, send_ask, 0)
-
-    def halo_copy(side):
-        peer = block + 1 - 2 * side
-        rows = pl.ds((1 - side) * (ROWS - HALO), HALO)
-        return pltpu.make_async_remote_copy(
-            sigma.at[rows], halo_in.at[side], halo_send.at[side], halo_recv.at[side],
-            device_id=(orbit, peer // 4, peer % 4), device_id_type=MESH,
-        )
-
     loads[3].wait()
-    has_side = (block > 0, block < TRAINERS - 1)
-    for side in range(2):
-
-        @pl.when(has_side[1 - side])
-        def _():
-            halo_copy(side).start()
-
-        @pl.when(jnp.logical_not(has_side[side]))
-        def _():
-            halo_in[side] = jnp.zeros((HALO, PIX), BF16)
 
     near = mask(jnp.abs(iota((PIX, PIX), 0) - iota((PIX, PIX), 1)) < 4.0)
 
@@ -170,7 +151,54 @@
         row = source_row[:, pl.ds(part * 128, 128)]
         source[pl.ds(part * 128, 128)] = jnp.transpose(jnp.broadcast_to(row, (128, 128)))
 
+    pl.semaphore_wait(barrier, OWNERS - 1 + 3 + 2)
+
+    pltpu.make_async_copy(ask_out.at[owner_of((orbit, scene))], ask_in.at[0], ask_recv.at[0]).start()
+
+    def send_ask(k, carry):
+        peer = plane(k, 1)
+        pltpu.make_async_remote_copy(
+            ask_out.at[owner_of(peer)], ask_in.at[k], ask_send, ask_recv.at[div(k, RG)],
+            device_id=peer, device_id_type=MESH,
+        ).start()
+        return carry
+
+    lax.fori_loop(1, OWNERS, send_ask, 0)
+
+    def halo_copy(side):
+        peer = block + 1 - 2 * side
+        rows = pl.ds((1 - side) * (ROWS - HALO), HALO)
+        return pltpu.make_async_remote_copy(
+            sigma.at[rows], halo_in.at[side], halo_send.at[side], halo_recv.at[side],
+            device_id=(orbit, div(peer, 4), rem(peer, 4)), device_id_type=MESH,
+        )
+
+    has_side = (block > 0, block < TRAINERS - 1)
+    for side in range(2):
+
+        @pl.when(has_side[1 - side])
+        def _():
+            halo_copy(side).start()
+
+        @pl.when(jnp.logical_not(has_side[side]))
+        def _():
+            halo_in[side] = jnp.zeros((HALO, PIX), BF16)
+
     loads[4].wait()
+
+    def reply(half, k):
+        step = div(k, PG[half])
+
+        @pl.when(k == 0)
+        def _():
+            pltpu.make_async_copy(rep_out.at[half, k], rep_in.at[half, k], rep_recv.at[half, step]).start()
+
+        @pl.when(k > 0)
+        def _():
+            pltpu.make_async_remote_copy(
+                rep_out.at[half, k], rep_in.at[half, k], rep_send.at[half], rep_recv.at[half, step],
+                device_id=plane(k, -1), device_id_type=MESH,
+            ).start()
 
     def gather_step(step, carry):
         group = pl.ds(step * RG, RG)
@@ -182,24 +210,20 @@
         column = jnp.concatenate(columns, axis=0)
         lane = iota((RG * CAPT, 128), 1)
         picker = jnp.concatenate([mask(column == lane + 128.0 * c) for c in range(ROWS // 128)], axis=1)
-        rep_out[group] = dot(picker, area[...]).astype(BF16).reshape(RG, CAPT, PIX)
+        picked = dot(picker, area[...]).astype(BF16)
+        for half in range(2):
+            rep_out[half, group] = picked[:, half * HALF : (half + 1) * HALF].reshape(RG, CAPT, HALF)
         for j in range(RG):
-            k = step * RG + j
-
-            @pl.when(k == 0)
-            def _():
-                pltpu.make_async_copy(rep_out.at[k], rep_in.at[k], rep_recv.at[step]).start()
-
-            @pl.when(k > 0)
-            def _():
-                pltpu.make_async_remote_copy(
-                    rep_out.at[k], rep_in.at[k], rep_send, rep_recv.at[step],
-                    device_id=plane(k, -1), device_id_type=MESH,
-                ).start()
-
+            reply(0, step * RG + j)
         return carry
 
     lax.fori_loop(0, OWNERS // RG, gather_step, 0)
+
+    def reply_rest(k, carry):
+        reply(1, k)
+        return carry
+
+    lax.fori_loop(0, OWNERS, reply_rest, 0)
 
     for device in column:
         pl.semaphore_signal(planes, inc=1, device_id=device, device_id_type=MESH)
@@ -240,64 +264,60 @@
 
     lax.fori_loop(0, ROWS // LEE, lee_step, 0)
 
-    def pick_step(step, carry):
-        group = pl.ds(step * RG, RG)
-        pltpu.make_async_copy(rep_in.at[group], rep_in.at[group], rep_recv.at[step]).wait()
-        table = rep_in[group].reshape(RG * CAPT, PIX)
-        firsts = [(owner_of(plane(step * RG + j, 1)) * CAPT).astype(F32) for j in range(RG)]
-        lane = iota((512, CAPT), 1)
-
-        def rows_step(part, inner):
-            rows = pl.ds(pl.multiple_of(part * 512, 512), 512)
-            column = source[rows]
-            picker = jnp.concatenate([mask(column == lane + first) for first in firsts], axis=1)
-            picked = dot(picker, table)
-            weight[rows] = jnp.where(step > 0, weight[rows] + picked, picked)
-            return inner
-
-        return lax.fori_loop(0, ROWS // 512, rows_step, carry)
-
-    weight[...] = jnp.zeros((ROWS, PIX), F32)
-    lax.fori_loop(0, OWNERS // RG, pick_step, 0)
-    pl.semaphore_wait(planes, 3)
-    flat[...] = (filtered[...] * weight[...]).astype(BF16)
-
-    def place_step(step, carry):
-        group = pl.ds(step * TG, TG)
+    def pick_step(half, step, carry):
+        group = pl.ds(step * PG[half], PG[half])
+        landed = rep_in.at[half, group]
+        pltpu.make_async_copy(landed, landed, rep_recv.at[half, step]).wait()
+        table = rep_in[half, group].reshape(PG[half] * CAPT, HALF)
+        firsts = [(owner_of(plane(step * PG[half] + j, 1)) * CAPT).astype(F32) for j in range(PG[half])]
+        lane = iota((ROWS, CAPT), 1)
+        column = source[...]
+        picker = jnp.concatenate([mask(column == lane + first) for first in firsts], axis=1)
+        weight[...] = weight[...] + dot(picker, table)
+        return carry
+
+    def place_step(half, step, carry):
+        group = pl.ds(step * TG[half], TG[half])
         row = target_row[...]
         line = iota((CAPR, ROWS), 0)
         pickers = []
-        for j in range(TG):
-            first = (trainer_of(cube(step * TG + j, 1)) * CAPR).astype(F32)
+        for j in range(TG[half]):
+            first = (trainer_of(cube(step * TG[half] + j, 1)) * CAPR).astype(F32)
             pickers.append(mask(line == row - first))
         placed = dot(jnp.concatenate(pickers, axis=0), flat[...])
-        put_out[group] = placed.astype(BF16).reshape(TG, CAPR, PIX)
-        for j in range(TG):
-            k = step * TG + j
+        put_out[half, group] = placed.astype(BF16).reshape(TG[half], CAPR, HALF)
+        for j in range(TG[half]):
+            k = step * TG[half] + j
 
             @pl.when(k == 0)
             def _():
-                pltpu.make_async_copy(put_out.at[k], put_in.at[block], put_recv.at[0]).start()
+                pltpu.make_async_copy(put_out.at[half, k], put_in.at[half, block], put_recv.at[half]).start()
 
             @pl.when(k > 0)
             def _():
                 pltpu.make_async_remote_copy(
-                    put_out.at[k], put_in.at[block], put_send, put_recv.at[0],
+                    put_out.at[half, k], put_in.at[half, block], put_send.at[half], put_recv.at[half],
                     device_id=cube(k, 1), device_id_type=MESH,
                 ).start()
 
         return carry
 
-    lax.fori_loop(0, TRAINERS // TG, place_step, 0)
-
-    pltpu.make_async_copy(put_in, put_in, put_recv.at[0]).wait()
-
-    for buffer, sem, count in (
-        (ask_out, ask_send, OWNERS - 1),
-        (rep_out, rep_send, OWNERS - 1),
-        (put_out, put_send, TRAINERS - 1),
-    ):
-        part = buffer.at[pl.ds(1, count)]
+    for half in range(2):
+        weight[...] = jnp.zeros((ROWS, HALF), F32)
+        lax.fori_loop(0, OWNERS // PG[half], functools.partial(pick_step, half), 0)
+        if half == 0:
+            pl.semaphore_wait(planes, 3)
+        flat[...] = (filtered[:, half * HALF : (half + 1) * HALF] * weight[...]).astype(BF16)
+        lax.fori_loop(0, TRAINERS // TG[half], functools.partial(place_step, half), 0)
+
+    for half in range(2):
+        pltpu.make_async_copy(put_in.at[half], put_in.at[half], put_recv.at[half]).wait()
+
+    sent = [(ask_out.at[pl.ds(1, OWNERS - 1)], ask_send)]
+    for half in range(2):
+        sent.append((rep_out.at[half, pl.ds(1, OWNERS - 1)], rep_send.at[half]))
+        sent.append((put_out.at[half, pl.ds(1, TRAINERS - 1)], put_send.at[half]))
+    for part, sem in sent:
         pltpu.make_async_copy(part, part, sem).wait()
     for side in range(2):
 
@@ -308,11 +328,14 @@
 
 def log_body(values, patches, logs, sems):
     copies = []
-    for step in range(TRAINERS // TG):
-        rows = pl.ds(step * TG * CAPR, TG * CAPR)
-        value = values[pl.ds(step * TG, TG)].reshape(TG * CAPR, PIX).astype(F32)
-        filled = value > 0.0
-        logs[rows] = jnp.where(filled, jnp.log(jnp.where(filled, value, 1.0)), 0.0)
+    for step in range(TRAINERS // LOG):
+        rows = pl.ds(step * LOG * CAPR, LOG * CAPR)
+        for half in range(2):
+            value = values[half, pl.ds(step * LOG, LOG)].reshape(LOG * CAPR, HALF).astype(F32)
+            filled = value > 0.0
+            logs[rows, half * HALF : (half + 1) * HALF] = jnp.where(
+                filled, jnp.log(jnp.where(filled, value, 1.0)), 0.0
+            )
         copies.append(pltpu.make_async_copy(logs.at[rows], patches.at[rows], sems.at[step]))
         copies[-1].start()
     for copy in copies:
@@ -325,7 +348,7 @@
     hbm = pl.BlockSpec(memory_space=pltpu.HBM)
     arrived = pl.pallas_call(
         body,
-        out_shape=jax.ShapeDtypeStruct((TRAINERS, CAPR, PIX), BF16),
+        out_shape=jax.ShapeDtypeStruct((2, TRAINERS, CAPR, HALF), BF16),
         in_specs=[hbm] * 5 + [vmem],
         out_specs=vmem,
         scratch_shapes=[
@@ -338,25 +361,25 @@
             pltpu.VMEM((ROWS + 2 * HALO, PIX), F32),
             pltpu.VMEM((ROWS + 2 * HALO, PIX), F32),
             pltpu.VMEM((ROWS, PIX), F32),
-            pltpu.VMEM((ROWS, PIX), F32),
-            pltpu.VMEM((ROWS, PIX), BF16),
+            pltpu.VMEM((ROWS, HALF), F32),
+            pltpu.VMEM((ROWS, HALF), BF16),
             pltpu.VMEM((ROWS, 128), F32),
             pltpu.VMEM((1, ROWS), F32),
             pltpu.VMEM((1, ROWS), F32),
             pltpu.VMEM((OWNERS, 1, CAPT), jnp.int32),
             pltpu.VMEM((OWNERS, 1, CAPT), jnp.int32),
-            pltpu.VMEM((OWNERS, CAPT, PIX), BF16),
-            pltpu.VMEM((OWNERS, CAPT, PIX), BF16),
-            pltpu.VMEM((TRAINERS, CAPR, PIX), BF16),
+            pltpu.VMEM((2, OWNERS, CAPT, HALF), BF16),
+            pltpu.VMEM((2, OWNERS, CAPT, HALF), BF16),
+            pltpu.VMEM((2, TRAINERS, CAPR, HALF), BF16),
             pltpu.VMEM((2, HALO, PIX), BF16),
             dma((2,)),
             dma((2,)),
             dma(()),
             dma((OWNERS // RG,)),
-            dma(()),
-            dma((OWNERS // RG,)),
-            dma(()),
-            dma((1,)),
+            dma((2,)),
+            dma((2, OWNERS // min(PG))),
+            dma((2,)),
+            dma((2,)),
             pltpu.SemaphoreType.REGULAR,
         ],
         compiler_params=pltpu.CompilerParams(
@@ -381,7 +404,7 @@
         out_shape=jax.ShapeDtypeStruct((TRAINERS * CAPR, PIX), F32),
         in_specs=[vmem],
         out_specs=hbm,
-        scratch_shapes=[pltpu.VMEM((TRAINERS * CAPR, PIX), F32), dma((TRAINERS // TG,))],
+        scratch_shapes=[pltpu.VMEM((TRAINERS * CAPR, PIX), F32), dma((TRAINERS // LOG,))],
         compiler_params=pltpu.CompilerParams(vmem_limit_bytes=16 << 20),
     )(arrived)
     return patches[None]

time: 74.2 us -> 67 us (0.903)
  Pallas kernels: 73.4 us -> 66.3 us
    pallas_call x1, Pallas kernels: 71.3 us -> 64.1 us  [per_device(): pl.pallas_call(body, out_shape=jax.ShapeDtypeStruct((2, TRAINERS, CAPR, H...]
where the time goes in v3:
time: 67 us; the launch traced here: 66.9 us
  Pallas kernels  66.3 us (99%)
    pallas_call x1, Pallas kernels, per_device(): pl.pallas_call(body, out_shape=jax.ShapeDtypeStruct((2, TRAINERS, CAPR, H...  64.1 us
    pallas_call x1, Pallas kernels, per_device(): pl.pallas_call(log_body, out_shape=jax.ShapeDtypeStruct((TRAINERS * CAPR,...  2.18 us

profile of v3, /device:TPU:1, one launch (start us, length us, event | category | flops | bytes accessed | tf_op | source)
XLA Modules:
  0.0 66.9 jit_solution(8555683631853786413)
XLA Ops:
  0.7 64.1 %shard_map.64.values = bf16[2,64,64,128]{3,2,1,0:T(8,128)(2,1)S(1)} custom-call(bf16[2048,256]{1,0:T(8,128)(2,1)} %bitcast.4, bf16[2048,256]{1,0:T(8,128)(2,1)} %area_hbm.1, s32[1,2048]{1,0:T(1,128)} %bitcast.5, s32[1,2048]{1,0:T(1,128)} %slot_hbm.1, s32[1,2048]{1,0:T(1,128)} %bitcast.6, s32[1,1]{1,0:T(1,128)S(6)} %copy.7.seam), custom_call_target="tpu_custom_call" | custom-call | flops 17179869184 | bytes 8388608 | tf_op jit(solution)/shard_map/pallas_call | solution.py:349
  64.8 2.2 %shard_map.65 = f32[4096,256]{1,0:T(8,128)} custom-call(bf16[2,64,64,128]{3,2,1,0:T(8,128)(2,1)S(1)} %shard_map.64.values), custom_call_target="tpu_custom_call" | custom-call | tf_op jit(solution)/shard_map/pallas_call | solution.py:402

commit v4 on v3

--- a/solution.py
+++ b/solution.py
@@ -17,7 +17,7 @@
 RG = 4
 PG = (8, 4)
 TG = (16, 8)
-LOG = 8
+LOG = 4
 HALO = 16
 HALF = PIX // 2
 LEE = 64
@@ -73,6 +73,30 @@
     def trainer_of(device):
         return device[1] * 4 + device[2]
 
+    barrier = pltpu.get_barrier_semaphore()
+
+    def greet(device):
+        pl.semaphore_signal(barrier, inc=1, device_id=device, device_id_type=MESH)
+
+    orbits = [rem(orbit + d, 2) for d in range(2)]
+    rows_of = [rem(y + d, 4) * 4 for d in range(4)]
+    columns_of = [rem(x + d, 4) for d in range(4)]
+
+    def at(offset):
+        return (orbits[offset % 2], rows_of[offset // 8] + columns_of[offset // 2 % 4], shard)
+
+    def hops(offset):
+        return -sum(min(d, 4 - d) for d in (offset // 8, offset // 2 % 4))
+
+    for offset in sorted(range(1, OWNERS), key=hops):
+        greet(at(offset))
+    column = [(orbit, scene, rem(shard + d, 4)) for d in range(1, 4)]
+    for device in column:
+        greet(device)
+    for side in (1, TRAINERS - 1):
+        peer = rem(block + side, TRAINERS)
+        greet((orbit, div(peer, 4), rem(peer, 4)))
+
     loads = [
         pltpu.make_async_copy(*ends, loaded.at[index])
         for index, ends in enumerate(
@@ -81,23 +105,6 @@
     ]
     for load in loads:
         load.start()
-
-    barrier = pltpu.get_barrier_semaphore()
-
-    def greet(device):
-        pl.semaphore_signal(barrier, inc=1, device_id=device, device_id_type=MESH)
-
-    def greet_plane(k, carry):
-        greet(plane(k, 1))
-        return carry
-
-    lax.fori_loop(1, OWNERS, greet_plane, 0)
-    column = [(orbit, scene, rem(shard + d, 4)) for d in range(1, 4)]
-    for device in column:
-        greet(device)
-    for side in (1, TRAINERS - 1):
-        peer = rem(block + side, TRAINERS)
-        greet((orbit, div(peer, 4), rem(peer, 4)))
 
     for load in loads[:3]:
         load.wait()
@@ -129,7 +136,39 @@
     for index in range(OWNERS):
         ask_out[index] = positions[index : index + 1, :]
 
+    pl.semaphore_wait(barrier, OWNERS - 1 + 3 + 2)
+
+    pltpu.make_async_copy(ask_out.at[owner_of((orbit, scene))], ask_in.at[0], ask_recv.at[0]).start()
+
+    def send_ask(k, carry):
+        peer = plane(k, 1)
+        pltpu.make_async_remote_copy(
+            ask_out.at[owner_of(peer)], ask_in.at[k], ask_send, ask_recv.at[div(k, RG)],
+            device_id=peer, device_id_type=MESH,
+        ).start()
+        return carry
+
+    lax.fori_loop(1, OWNERS, send_ask, 0)
+
+    def halo_copy(side):
+        peer = block + 1 - 2 * side
+        rows = pl.ds((1 - side) * (ROWS - HALO), HALO)
+        return pltpu.make_async_remote_copy(
+            sigma.at[rows], halo_in.at[side], halo_send.at[side], halo_recv.at[side],
+            device_id=(orbit, div(peer, 4), rem(peer, 4)), device_id_type=MESH,
+        )
+
     loads[3].wait()
+    has_side = (block > 0, block < TRAINERS - 1)
+    for side in range(2):
+
+        @pl.when(has_side[1 - side])
+        def _():
+            halo_copy(side).start()
+
+        @pl.when(jnp.logical_not(has_side[side]))
+        def _():
+            halo_in[side] = jnp.zeros((HALO, PIX), BF16)
 
     near = mask(jnp.abs(iota((PIX, PIX), 0) - iota((PIX, PIX), 1)) < 4.0)
 
@@ -146,43 +185,6 @@
         return carry
 
     lax.fori_loop(0, ROWS // 256, sums_step, 0)
-
-    for part in range(ROWS // 128):
-        row = source_row[:, pl.ds(part * 128, 128)]
-        source[pl.ds(part * 128, 128)] = jnp.transpose(jnp.broadcast_to(row, (128, 128)))
-
-    pl.semaphore_wait(barrier, OWNERS - 1 + 3 + 2)
-
-    pltpu.make_async_copy(ask_out.at[owner_of((orbit, scene))], ask_in.at[0], ask_recv.at[0]).start()
-
-    def send_ask(k, carry):
-        peer = plane(k, 1)
-        pltpu.make_async_remote_copy(
-            ask_out.at[owner_of(peer)], ask_in.at[k], ask_send, ask_recv.at[div(k, RG)],
-            device_id=peer, device_id_type=MESH,
-        ).start()
-        return carry
-
-    lax.fori_loop(1, OWNERS, send_ask, 0)
-
-    def halo_copy(side):
-        peer = block + 1 - 2 * side
-        rows = pl.ds((1 - side) * (ROWS - HALO), HALO)
-        return pltpu.make_async_remote_copy(
-            sigma.at[rows], halo_in.at[side], halo_send.at[side], halo_recv.at[side],
-            device_id=(orbit, div(peer, 4), rem(peer, 4)), device_id_type=MESH,
-        )
-
-    has_side = (block > 0, block < TRAINERS - 1)
-    for side in range(2):
-
-        @pl.when(has_side[1 - side])
-        def _():
-            halo_copy(side).start()
-
-        @pl.when(jnp.logical_not(has_side[side]))
-        def _():
-            halo_in[side] = jnp.zeros((HALO, PIX), BF16)
 
     loads[4].wait()
 
@@ -264,6 +266,11 @@
 
     lax.fori_loop(0, ROWS // LEE, lee_step, 0)
 
+    for part in range(ROWS // 128):
+        row = source_row[:, pl.ds(part * 128, 128)]
+        source[pl.ds(part * 128, 128)] = jnp.transpose(jnp.broadcast_to(row, (128, 128)))
+
+
     def pick_step(half, step, carry):
         group = pl.ds(step * PG[half], PG[half])
         landed = rep_in.at[half, group]
@@ -332,10 +339,7 @@
         rows = pl.ds(step * LOG * CAPR, LOG * CAPR)
         for half in range(2):
             value = values[half, pl.ds(step * LOG, LOG)].reshape(LOG * CAPR, HALF).astype(F32)
-            filled = value > 0.0
-            logs[rows, half * HALF : (half + 1) * HALF] = jnp.where(
-                filled, jnp.log(jnp.where(filled, value, 1.0)), 0.0
-            )
+            logs[rows, half * HALF : (half + 1) * HALF] = jnp.where(value > 0.0, jnp.log(value), 0.0)
         copies.append(pltpu.make_async_copy(logs.at[rows], patches.at[rows], sems.at[step]))
         copies[-1].start()
     for copy in copies:

time: 67 us -> 65.6 us (0.979)
  Pallas kernels: 66.3 us -> 64.7 us
    pallas_call x1, Pallas kernels: 64.1 us -> 62.5 us  [per_device(): pl.pallas_call(body, out_shape=jax.ShapeDtypeStruct((2, TRAINERS, CAPR, H...]
where the time goes in v4:
time: 65.6 us; the launch traced here: 65.4 us
  Pallas kernels  64.7 us (99%)
  between operations  0.66 us (1%)
    pallas_call x1, Pallas kernels, per_device(): pl.pallas_call(body, out_shape=jax.ShapeDtypeStruct((2, TRAINERS, CAPR, H...  62.5 us
    pallas_call x1, Pallas kernels, per_device(): pl.pallas_call(log_body, out_shape=jax.ShapeDtypeStruct((TRAINERS * CAPR,...  2.18 us

profile of v4, /device:TPU:1, one launch (start us, length us, event | category | flops | bytes accessed | tf_op | source)
XLA Modules:
  0.0 65.4 jit_solution(5984195803110983630)
XLA Ops:
  0.7 62.5 %shard_map.64.values = bf16[2,64,64,128]{3,2,1,0:T(8,128)(2,1)S(1)} custom-call(bf16[2048,256]{1,0:T(8,128)(2,1)} %bitcast.4, bf16[2048,256]{1,0:T(8,128)(2,1)} %area_hbm.1, s32[1,2048]{1,0:T(1,128)} %bitcast.5, s32[1,2048]{1,0:T(1,128)} %slot_hbm.1, s32[1,2048]{1,0:T(1,128)} %bitcast.6, s32[1,1]{1,0:T(1,128)S(6)} %copy.7.seam), custom_call_target="tpu_custom_call" | custom-call | flops 17179869184 | bytes 8388608 | tf_op jit(solution)/shard_map/pallas_call | solution.py:353
  63.2 2.2 %shard_map.65 = f32[4096,256]{1,0:T(8,128)} custom-call(bf16[2,64,64,128]{3,2,1,0:T(8,128)(2,1)S(1)} %shard_map.64.values), custom_call_target="tpu_custom_call" | custom-call | tf_op jit(solution)/shard_map/pallas_call | solution.py:406

commit v5 on v4

--- a/solution.py
+++ b/solution.py
@@ -14,9 +14,9 @@
 CAPT = 128
 TRAINERS = 64
 CAPR = 64
-RG = 4
+RG = 2
 PG = (8, 4)
-TG = (16, 8)
+TG = (16, 4)
 LOG = 4
 HALO = 16
 HALF = PIX // 2

time: 65.6 us -> 65.4 us (level)
  no operation moved by 1% of the time
where the time goes in v5:
time: 65.4 us; the launch traced here: 65.1 us
  Pallas kernels  64.4 us (98%)
  between operations  0.66 us (1%)
    pallas_call x1, Pallas kernels, per_device(): pl.pallas_call(body, out_shape=jax.ShapeDtypeStruct((2, TRAINERS, CAPR, H...  62.3 us
    pallas_call x1, Pallas kernels, per_device(): pl.pallas_call(log_body, out_shape=jax.ShapeDtypeStruct((TRAINERS * CAPR,...  2.18 us

profile of v5, /device:TPU:1, one launch (start us, length us, event | category | flops | bytes accessed | tf_op | source)
XLA Modules:
  0.0 65.1 jit_solution(16002544887364912355)
XLA Ops:
  0.7 62.3 %shard_map.64.values = bf16[2,64,64,128]{3,2,1,0:T(8,128)(2,1)S(1)} custom-call(bf16[2048,256]{1,0:T(8,128)(2,1)} %bitcast.4, bf16[2048,256]{1,0:T(8,128)(2,1)} %area_hbm.1, s32[1,2048]{1,0:T(1,128)} %bitcast.5, s32[1,2048]{1,0:T(1,128)} %slot_hbm.1, s32[1,2048]{1,0:T(1,128)} %bitcast.6, s32[1,1]{1,0:T(1,128)S(6)} %copy.7.seam), custom_call_target="tpu_custom_call" | custom-call | flops 17179869184 | bytes 8388608 | tf_op jit(solution)/shard_map/pallas_call | solution.py:353
  62.9 2.2 %shard_map.65 = f32[4096,256]{1,0:T(8,128)} custom-call(bf16[2,64,64,128]{3,2,1,0:T(8,128)(2,1)S(1)} %shard_map.64.values), custom_call_target="tpu_custom_call" | custom-call | tf_op jit(solution)/shard_map/pallas_call | solution.py:406

commit v6 on v5

--- a/solution.py
+++ b/solution.py
@@ -16,7 +16,7 @@
 CAPR = 64
 RG = 2
 PG = (8, 4)
-TG = (16, 4)
+TG = (32, 4)
 LOG = 4
 HALO = 16
 HALF = PIX // 2

time: 65.4 us -> 65.4 us (level)
  no operation moved by 1% of the time
where the time goes in v6:
time: 65.4 us; the launch traced here: 65.1 us
  Pallas kernels  64.4 us (98%)
  between operations  0.66 us (1%)
    pallas_call x1, Pallas kernels, per_device(): pl.pallas_call(body, out_shape=jax.ShapeDtypeStruct((2, TRAINERS, CAPR, H...  62.3 us
    pallas_call x1, Pallas kernels, per_device(): pl.pallas_call(log_body, out_shape=jax.ShapeDtypeStruct((TRAINERS * CAPR,...  2.18 us

profile of v6, /device:TPU:1, one launch (start us, length us, event | category | flops | bytes accessed | tf_op | source)
XLA Modules:
  0.0 65.1 jit_solution(18415781686013735069)
XLA Ops:
  0.7 62.3 %shard_map.64.values = bf16[2,64,64,128]{3,2,1,0:T(8,128)(2,1)S(1)} custom-call(bf16[2048,256]{1,0:T(8,128)(2,1)} %bitcast.4, bf16[2048,256]{1,0:T(8,128)(2,1)} %area_hbm.1, s32[1,2048]{1,0:T(1,128)} %bitcast.5, s32[1,2048]{1,0:T(1,128)} %slot_hbm.1, s32[1,2048]{1,0:T(1,128)} %bitcast.6, s32[1,1]{1,0:T(1,128)S(6)} %copy.7.seam), custom_call_target="tpu_custom_call" | custom-call | flops 17179869184 | bytes 8388608 | tf_op jit(solution)/shard_map/pallas_call | solution.py:353
  62.9 2.2 %shard_map.65 = f32[4096,256]{1,0:T(8,128)} custom-call(bf16[2,64,64,128]{3,2,1,0:T(8,128)(2,1)S(1)} %shard_map.64.values), custom_call_target="tpu_custom_call" | custom-call | tf_op jit(solution)/shard_map/pallas_call | solution.py:406
